TPU v7x, 32 devices: a whole 2x2x4 slice. The times are simulated.
32 devices in a mesh: slab: 8 (over z, y), grp: 4 (over x, core).
Axes of the slice: x: 2, y: 2, z: 4, core: 2. Of those that a mesh axis runs over, the one named last changes fastest.
Arguments:
- positions: float32 [32, 16, 3, 128], P('slab', 'grp'), may hold values from 0 to 1
- sketch: bfloat16 [32, 16, 128, 256], P('slab', 'grp'), may hold values from -6 to 6
- counts: int32 [32, 16], P('slab', 'grp'), may hold values from 32 to 128, as said below
- neighbours: int32 [32, 16, 8], P('slab', 'grp'), may hold values from 0 to 8, as said below
Outputs:
- basis: bfloat16 [32, 16, 128, 256], P('slab', 'grp')
- factor: float32 [256, 256], replicated
Inputs may be any that keep to these rules, and one draw needn't show every extreme that they name: `counts`: the first block of every device's region of 4 x 4 blocks is full. `neighbours`: a code is 3 (dz + 1) + (dy + 1) for offsets dz, dy in -1, 0, 1; the codes of one block are distinct and always include 4 (the block itself); each block leaves out exactly one of its nine codes, and the lists are symmetric: block a lists block b if and only if block b lists block a; the left-out pairs lie inside aligned 2 x 2 squares of blocks.
All inputs are finite; a program needn't handle non-finite values.
Results may differ from a plain program's by a relative error of at most 0.017.
Values may be sent and summed in bfloat16 or wider, within the bound.
A program may use at most 64 MiB of HBM per device.

v0:
```python
import math

import jax
import jax.numpy as jnp
from jax import lax
from jax.sharding import PartitionSpec as P


def padded(shard, sides, width):
    for axis, dim in sides:
        count, length = (lax.axis_size(axis), shard.shape[dim])
        up = [(i, (i + 1) % count) for i in range(count)]
        down = [(j, i) for i, j in up]
        last = lax.slice_in_dim(shard, length - width, length, axis=dim)
        leading = lax.slice_in_dim(shard, 0, width, axis=dim)
        before = lax.ppermute(last, axis, up)
        after = lax.ppermute(leading, axis, down)
        shard = jnp.concatenate([before, shard, after], axis=dim)
    return shard


def kernel_tile(own_pos, other_pos, shift_z, shift_y):
    diff_z = other_pos[..., 0, None, :] + shift_z[..., None, None] - own_pos[..., 0, :, None]
    diff_y = other_pos[..., 1, None, :] + shift_y[..., None, None] - own_pos[..., 1, :, None]
    diff_x = other_pos[..., 2, None, :] - own_pos[..., 2, :, None]
    radius = jnp.sqrt(diff_z * diff_z + diff_y * diff_y + diff_x * diff_x)
    taper = jnp.maximum(1.0 - radius, 0.0)
    return taper**4 * (4.0 * radius + 1.0)


def on_device(positions, sketch, counts, neighbours):
    blocks_z, blocks_y, _, points = positions.shape
    columns = sketch.shape[3]
    live_mask = (
        lax.broadcasted_iota(jnp.int32, (blocks_z, blocks_y, points), 2) < counts[:, :, None]
    )
    masked = jnp.where(live_mask[..., None], sketch, jnp.zeros_like(sketch))
    wide_pos, wide_rows = (
        padded(positions.astype(jnp.bfloat16), (("slab", 0), ("grp", 1)), 1).astype(
            positions.dtype
        ),
        padded(masked, (("slab", 0), ("grp", 1)), 1),
    )
    pos_table = wide_pos.reshape(-1, 3, points)
    row_table = wide_rows.reshape(-1, points, columns)
    own_pos = positions.reshape(-1, 3, points)
    row_ids = lax.broadcasted_iota(jnp.int32, (blocks_z, blocks_y), 0)
    col_ids = lax.broadcasted_iota(jnp.int32, (blocks_z, blocks_y), 1)
    image = jnp.zeros((blocks_z * blocks_y, points, columns), jnp.float32)
    for slot_index in range(neighbours.shape[2]):
        offset_code = neighbours[:, :, slot_index]
        shift_z = offset_code // 3 - 1
        shift_y = offset_code % 3 - 1
        source_ids = ((row_ids + 1 + shift_z) * (blocks_y + 2) + col_ids + 1 + shift_y).reshape(-1)
        other_pos = jnp.take(pos_table, source_ids, axis=0)
        other_rows = jnp.take(row_table, source_ids, axis=0)
        weights = kernel_tile(
            own_pos,
            other_pos,
            shift_z.reshape(-1).astype(jnp.float32),
            shift_y.reshape(-1).astype(jnp.float32),
        ).astype(jnp.bfloat16)
        image = image + jnp.einsum(
            "bij,bjr->bir", weights, other_rows, preferred_element_type=jnp.float32
        )
    image = jnp.where(live_mask.reshape(-1, points)[..., None], image, jnp.zeros_like(image))
    flat_rows = image.reshape(-1, columns)
    gram_local = jnp.dot(
        flat_rows.T, flat_rows, preferred_element_type=jnp.float32, precision=lax.Precision.HIGHEST
    )
    gram_total = lax.psum(gram_local, ("slab", "grp"))
    lower_factor = jnp.linalg.cholesky(gram_total)
    solved = lax.linalg.triangular_solve(lower_factor, flat_rows.T, left_side=True, lower=True)
    total_rows = lax.axis_size("slab") * blocks_z * lax.axis_size("grp") * blocks_y * points
    scale_rows = math.sqrt(total_rows)
    basis = (
        (solved.T * scale_rows).reshape(blocks_z, blocks_y, points, columns).astype(jnp.bfloat16)
    )
    factor = lower_factor.T / scale_rows
    return (basis, factor)


def solution(mesh):
    placed = (
        P("slab", "grp", None, None),
        P("slab", "grp", None, None),
        P("slab", "grp"),
        P("slab", "grp", None),
    )
    return jax.shard_map(
        on_device,
        mesh=mesh,
        in_specs=placed,
        out_specs=(P("slab", "grp", None, None), P()),
        check_vma=False,
    )
```

profile of v0, /device:TPU:1, one launch (start us, length us, event | category | flops | bytes accessed | tf_op | source)
XLA Modules:
  0.0 278.6 jit_solution(16708323109046703102)
XLA Ops:
  8.0 2.1 collective-permute-start
  10.1 3.1 %collective-permute-start.1 = (bf16[1,4,3,128]{3,1,2,0:T(4,128)(2,1)S(1)}, bf16[1,4,3,128]{3,1,2,0:T(4,128)(2,1)S(1)}, u32[]{:S(2)}, u32[]{:S(2)}) collective-permute-start(bf16[1,4,3,128]{3,1,2,0:T(4,128)(2,1)S(1)} %get-tuple-element.122), channel_id=1, source_target_pairs={{4,0},{8,4},{12,8},{16,12},{20,16},{24,20},{28,24},{0,28},{5,1},{9... | collective-permute-start | bytes 9224 | tf_op jit(solution)/shard_map/ppermute | solution.py:17
  14.0 1.5 broadcast_select_fusion
  15.6 4.1 %collective-permute-start.5 = (bf16[1,4,128,256]{3,2,1,0:T(8,128)(2,1)S(1)}, bf16[1,4,128,256]{3,2,1,0:T(8,128)(2,1)S(1)}, u32[]{:S(2)}, u32[]{:S(2)}) collective-permute-start(bf16[1,4,128,256]{3,2,1,0:T(8,128)(2,1)S(1)} %get-tuple-element.85), channel_id=1, source_target_pairs={{4,0},{8,4},{12,8},{16,12},{20,16},{24,20},{28,24},{0,28},{5,1},{9... | collective-permute-start | bytes 786440 | tf_op jit(solution)/shard_map/ppermute | solution.py:17
  24.7 2.8 collective-permute-start.2
  28.3 2.3 collective-permute-done.3
  39.8 6.2 %collective-permute-done.6 = bf16[6,1,128,256]{3,2,1,0:T(8,128)(2,1)S(1)} collective-permute-done((bf16[6,1,128,256]{3,2,1,0:T(8,128)(2,1)S(1)}, bf16[6,1,128,256]{3,2,1,0:T(8,128)(2,1)S(1)}, u32[]{:S(2)}, u32[]{:S(2)}) %collective-permute-start.6) | collective-permute-done | bytes 393248 | tf_op jit(solution)/shard_map/ppermute | solution.py:16
  46.0 1.5 collective-permute-done.7
  47.5 1.4 pad_maximum_fusion
  49.5 1.7 gather_fusion.13
  51.2 1.7 gather_fusion.11
  52.9 1.7 gather_fusion.9
  54.6 1.7 gather_fusion.7
  56.4 1.7 gather_fusion.5
  58.1 1.8 gather_fusion.3
  59.9 1.8 gather_fusion.1
  61.7 2.4 fusion.5
  64.2 1.7 fusion.7
  65.9 1.7 fusion.9
  67.7 1.7 fusion.11
  69.5 1.7 fusion.13
  71.3 1.7 fusion.17
  73.1 1.7 fusion.15
  74.8 2.8 add_select_fusion
  77.6 4.2 %convolution_bitcast_fusion = f32[256,256]{0,1:T(8,128)} fusion(f32[16,128,256]{2,1,0:T(8,128)S(1)} %add_select_fusion), kind=kOutput, calls=%fused_computation.23 | convolution fusion | flops 1610612736 | bytes 2359296 | tf_op jit(solution)/shard_map/dot_general | solution.py:68
  81.8 121.1 %all-reduce.3.cloned.1.call-done = f32[256,256]{0,1:T(8,128)} async-done(((f32[256,256]{0,1:T(8,128)}), f32[256,256]{0,1:T(8,128)}) %all-reduce.3.cloned.1.call-update) | async-done | bytes 262160 | tf_op jit(solution)/shard_map/psum | solution.py:71
  205.0 11.7 %cholesky.50 = f32[128,128]{1,0:T(8,128)S(1)} custom-call(f32[128,128]{1,0:T(8,128)S(1)} %cholesky.118), custom_call_target="Cholesky" | custom-call | tf_op jit(solution)/shard_map/jit(cholesky)/cholesky | solution.py:72
  217.4 9.8 %custom-call.14 = f32[1,128,128]{1,2,0:T(8,128)S(1)} custom-call(f32[1,128,128]{2,1,0:T(8,128)S(1)} %get-tuple-element.91), custom_call_target="InvertDiagBlocksLowerTriangular" | custom-call | tf_op jit(solution)/shard_map/jit(cholesky)/cholesky | solution.py:72
  227.7 11.9 %cholesky.105 = f32[128,128]{1,0:T(8,128)S(1)} custom-call(f32[128,128]{1,0:T(8,128)S(1)} %convolution_subtract_fusion.1), custom_call_target="Cholesky" | custom-call | tf_op jit(solution)/shard_map/jit(cholesky)/cholesky | solution.py:72
  242.6 4.0 %while.1 = (s32[]{:T(128)}, f32[256,256]{1,0:T(8,128)S(1)}, s32[2,2]{1,0:T(2,128)S(1)}, f32[2,128,128]{2,1,0:T(8,128)S(1)}, s32[]{:T(128)}) while((s32[]{:T(128)}, f32[256,256]{1,0:T(8,128)S(1)}, s32[2,2]{1,0:T(2,128)S(1)}, f32[2,128,128]{2,1,0:T(8,128)S(1)}, s32[]{:T(128)}) %tuple.117), condition=%wide.while_cond, body=%wide.while_body.sunk | while | flops 2 | bytes 131189 | solution.py:73
  246.6 19.7 %custom-call.15 = f32[2,128,128]{1,2,0:T(8,128)S(1)} custom-call(f32[2,128,128]{2,1,0:T(8,128)S(1)} %get-tuple-element.11), custom_call_target="InvertDiagBlocksLowerTriangular" | custom-call | tf_op jit(solution)/shard_map/triangular_solve | solution.py:73
  267.3 1.8 convolution_subtract_fusion
  (206 shorter events, 29.4 us)
Async XLA Ops:
  7.2 12.7 %copy-start.9 = (f32[4,4,3,128]{3,1,2,0:T(4,128)S(1)}, f32[4,4,3,128]{3,1,2,0:T(4,128)}, u32[]{:S(2)}) copy-start(f32[4,4,3,128]{3,1,2,0:T(4,128)} %param.8) | copy-start | bytes 73732
  7.2 12.6 %copy-start.20 = (s32[4,4]{1,0:T(4,128)S(1)}, s32[4,4]{1,0:T(4,128)}, u32[]{:S(2)}) copy-start(s32[4,4]{1,0:T(4,128)} %param.10) | copy-start | bytes 196
  7.2 12.6 %copy-start = (s32[4,4,8]{2,1,0:T(4,128)S(1)}, s32[4,4,8]{2,1,0:T(4,128)}, u32[]{:S(2)}) copy-start(s32[4,4,8]{2,1,0:T(4,128)} %param.11) | copy-start | bytes 1540
  7.2 195.7 %all-reduce.3.cloned.1.call-start = ((), (), s32[]{:S(2)}) async-start(), calls=%async_computation | async-start | bytes 524288 | tf_op jit(solution)/shard_map/psum | solution.py:71
  8.0 16.6 %collective-permute-start = (bf16[1,4,3,128]{3,1,2,0:T(4,128)(2,1)S(1)}, bf16[1,4,3,128]{3,1,2,0:T(4,128)(2,1)S(1)}, u32[]{:S(2)}, u32[]{:S(2)}) collective-permute-start(bf16[1,4,3,128]{3,1,2,0:T(4,128)(2,1)S(1)} %get-tuple-element.121), channel_id=1, source_target_pairs={{0,4},{4,8},{8,12},{12,16},{16,20},{20,24},{24,28},{28,0},{1,5},{5... | collective-permute-start | bytes 9224 | tf_op jit(solution)/shard_map/ppermute | solution.py:16
  10.1 14.5 %collective-permute-start.1 = (bf16[1,4,3,128]{3,1,2,0:T(4,128)(2,1)S(1)}, bf16[1,4,3,128]{3,1,2,0:T(4,128)(2,1)S(1)}, u32[]{:S(2)}, u32[]{:S(2)}) collective-permute-start(bf16[1,4,3,128]{3,1,2,0:T(4,128)(2,1)S(1)} %get-tuple-element.122), channel_id=1, source_target_pairs={{4,0},{8,4},{12,8},{16,12},{20,16},{24,20},{28,24},{0,28},{5,1},{9... | collective-permute-start | bytes 9224 | tf_op jit(solution)/shard_map/ppermute | solution.py:17
  15.5 22.2 %collective-permute-start.4 = (bf16[1,4,128,256]{3,2,1,0:T(8,128)(2,1)S(1)}, bf16[1,4,128,256]{3,2,1,0:T(8,128)(2,1)S(1)}, u32[]{:S(2)}, u32[]{:S(2)}) collective-permute-start(bf16[1,4,128,256]{3,2,1,0:T(8,128)(2,1)S(1)} %get-tuple-element.84), channel_id=1, source_target_pairs={{0,4},{4,8},{8,12},{12,16},{16,20},{20,24},{24,28},{28,0},{1,5},{5... | collective-permute-start | bytes 786440 | tf_op jit(solution)/shard_map/ppermute | solution.py:16
  15.6 22.1 %collective-permute-start.5 = (bf16[1,4,128,256]{3,2,1,0:T(8,128)(2,1)S(1)}, bf16[1,4,128,256]{3,2,1,0:T(8,128)(2,1)S(1)}, u32[]{:S(2)}, u32[]{:S(2)}) collective-permute-start(bf16[1,4,128,256]{3,2,1,0:T(8,128)(2,1)S(1)} %get-tuple-element.85), channel_id=1, source_target_pairs={{4,0},{8,4},{12,8},{16,12},{20,16},{24,20},{28,24},{0,28},{5,1},{9... | collective-permute-start | bytes 786440 | tf_op jit(solution)/shard_map/ppermute | solution.py:17
  24.4 10.0 %copy-start.28 = (pred[16]{0:T(512)(128)(4,1)}, pred[16]{0:T(512)(128)(4,1)S(1)}, u32[]{:S(2)}) copy-start(pred[16]{0:T(512)(128)(4,1)S(1)} %get-tuple-element.50) | copy-start | bytes 52
  24.4 10.5 %copy-start.34 = (pred[16]{0:T(512)(128)(4,1)}, pred[16]{0:T(512)(128)(4,1)S(1)}, u32[]{:S(2)}) copy-start(pred[16]{0:T(512)(128)(4,1)S(1)} %get-tuple-element.131) | copy-start | bytes 52
  24.4 10.5 %copy-start.36 = (pred[16]{0:T(512)(128)(4,1)}, pred[16]{0:T(512)(128)(4,1)S(1)}, u32[]{:S(2)}) copy-start(pred[16]{0:T(512)(128)(4,1)S(1)} %get-tuple-element.129) | copy-start | bytes 52
  24.4 10.5 %copy-start.38 = (pred[16]{0:T(512)(128)(4,1)}, pred[16]{0:T(512)(128)(4,1)S(1)}, u32[]{:S(2)}) copy-start(pred[16]{0:T(512)(128)(4,1)S(1)} %get-tuple-element.127) | copy-start | bytes 52
  24.4 10.5 %copy-start.40 = (pred[16]{0:T(512)(128)(4,1)}, pred[16]{0:T(512)(128)(4,1)S(1)}, u32[]{:S(2)}) copy-start(pred[16]{0:T(512)(128)(4,1)S(1)} %get-tuple-element.125) | copy-start | bytes 52
  24.4 13.1 %copy-start.42 = (pred[16]{0:T(512)(128)(4,1)}, pred[16]{0:T(512)(128)(4,1)S(1)}, u32[]{:S(2)}) copy-start(pred[16]{0:T(512)(128)(4,1)S(1)} %get-tuple-element.123) | copy-start | bytes 52
  24.4 14.6 %copy-start.30 = (pred[16]{0:T(512)(128)(4,1)}, pred[16]{0:T(512)(128)(4,1)S(1)}, u32[]{:S(2)}) copy-start(pred[16]{0:T(512)(128)(4,1)S(1)} %get-tuple-element.133) | copy-start | bytes 52
  24.5 14.6 %copy-start.32 = (pred[16]{0:T(512)(128)(4,1)}, pred[16]{0:T(512)(128)(4,1)S(1)}, u32[]{:S(2)}) copy-start(pred[16]{0:T(512)(128)(4,1)S(1)} %get-tuple-element.135) | copy-start | bytes 52
  24.5 9.7 %copy-start.21 = (s32[1024]{0:T(1024)}, s32[1024]{0:T(1024)S(1)}, u32[]{:S(2)}) copy-start(s32[1024]{0:T(1024)S(1)} %pad_clamp_fusion.1) | copy-start | bytes 12292
  24.5 9.7 %copy-start.22 = (s32[1024]{0:T(1024)}, s32[1024]{0:T(1024)S(1)}, u32[]{:S(2)}) copy-start(s32[1024]{0:T(1024)S(1)} %pad_clamp_fusion.2) | copy-start | bytes 12292
  24.5 9.8 %copy-start.23 = (s32[1024]{0:T(1024)}, s32[1024]{0:T(1024)S(1)}, u32[]{:S(2)}) copy-start(s32[1024]{0:T(1024)S(1)} %pad_clamp_fusion.3) | copy-start | bytes 12292
  24.6 9.8 %copy-start.24 = (s32[1024]{0:T(1024)}, s32[1024]{0:T(1024)S(1)}, u32[]{:S(2)}) copy-start(s32[1024]{0:T(1024)S(1)} %pad_clamp_fusion.4) | copy-start | bytes 12292
  24.6 9.8 %copy-start.25 = (s32[1024]{0:T(1024)}, s32[1024]{0:T(1024)S(1)}, u32[]{:S(2)}) copy-start(s32[1024]{0:T(1024)S(1)} %pad_clamp_fusion.5) | copy-start | bytes 12292
  24.6 12.9 %copy-start.26 = (s32[1024]{0:T(1024)}, s32[1024]{0:T(1024)S(1)}, u32[]{:S(2)}) copy-start(s32[1024]{0:T(1024)S(1)} %pad_clamp_fusion.6) | copy-start | bytes 12292
  24.7 3.6 %collective-permute-start.2 = (bf16[6,1,3,128]{3,1,2,0:T(2,128)(2,1)S(1)}, bf16[6,1,3,128]{3,1,2,0:T(2,128)(2,1)S(1)}, u32[]{:S(2)}, u32[]{:S(2)}) collective-permute-start(bf16[6,1,3,128]{3,1,2,0:T(2,128)(2,1)S(1)} %get-tuple-element.119), channel_id=1, source_target_pairs={{0,1},{1,2},{2,3},{3,0},{4,5},{5,6},{6,7},{7,4},{8,9},{9,10},{10,1... | collective-permute-start | bytes 13832 | tf_op jit(solution)/shard_map/ppermute | solution.py:16
  27.5 3.1 %collective-permute-start.3 = (bf16[6,1,3,128]{3,1,2,0:T(2,128)(2,1)S(1)}, bf16[6,1,3,128]{3,1,2,0:T(2,128)(2,1)S(1)}, u32[]{:S(2)}, u32[]{:S(2)}) collective-permute-start(bf16[6,1,3,128]{3,1,2,0:T(2,128)(2,1)S(1)} %get-tuple-element.120), channel_id=1, source_target_pairs={{1,0},{2,1},{3,2},{0,3},{5,4},{6,5},{7,6},{4,7},{9,8},{10,9},{11,1... | collective-permute-start | bytes 13832 | tf_op jit(solution)/shard_map/ppermute | solution.py:17
  27.5 10.1 %copy-start.27 = (s32[1024]{0:T(1024)}, s32[1024]{0:T(1024)S(1)}, u32[]{:S(2)}) copy-start(s32[1024]{0:T(1024)S(1)} %pad_clamp_fusion.7) | copy-start | bytes 12292
  37.7 8.3 %copy-start.1 = (bf16[1,4,128,256]{3,2,1,0:T(8,128)(2,1)}, bf16[1,4,128,256]{3,2,1,0:T(8,128)(2,1)S(1)}, u32[]{:S(2)}) copy-start(bf16[1,4,128,256]{3,2,1,0:T(8,128)(2,1)S(1)} %collective-permute-done.4) | copy-start | bytes 786436
  37.7 8.3 %copy-start.2 = (bf16[1,4,128,256]{3,2,1,0:T(8,128)(2,1)}, bf16[1,4,128,256]{3,2,1,0:T(8,128)(2,1)S(1)}, u32[]{:S(2)}) copy-start(bf16[1,4,128,256]{3,2,1,0:T(8,128)(2,1)S(1)} %collective-permute-done.5) | copy-start | bytes 786436
  37.8 8.2 %collective-permute-start.6 = (bf16[6,1,128,256]{3,2,1,0:T(8,128)(2,1)S(1)}, bf16[6,1,128,256]{3,2,1,0:T(8,128)(2,1)S(1)}, u32[]{:S(2)}, u32[]{:S(2)}) collective-permute-start(bf16[6,1,128,256]{3,2,1,0:T(8,128)(2,1)S(1)} %get-tuple-element.82), channel_id=1, source_target_pairs={{0,1},{1,2},{2,3},{3,0},{4,5},{5,6},{6,7},{7,4},{8,9},{9,10},{10,1... | collective-permute-start | bytes 1179656 | tf_op jit(solution)/shard_map/ppermute | solution.py:16
  37.9 9.6 %collective-permute-start.7 = (bf16[6,1,128,256]{3,2,1,0:T(8,128)(2,1)S(1)}, bf16[6,1,128,256]{3,2,1,0:T(8,128)(2,1)S(1)}, u32[]{:S(2)}, u32[]{:S(2)}) collective-permute-start(bf16[6,1,128,256]{3,2,1,0:T(8,128)(2,1)S(1)} %get-tuple-element.83), channel_id=1, source_target_pairs={{1,0},{2,1},{3,2},{0,3},{5,4},{6,5},{7,6},{4,7},{9,8},{10,9},{11,1... | collective-permute-start | bytes 1179656 | tf_op jit(solution)/shard_map/ppermute | solution.py:17
  58.1 3.6 %copy-start.43 = (pred[16]{0:T(512)(128)(4,1)S(1)}, pred[16]{0:T(512)(128)(4,1)}, u32[]{:S(2)}) copy-start(pred[16]{0:T(512)(128)(4,1)} %copy-done.42) | copy-start | bytes 52
  61.7 2.4 copy-start.8
  61.7 2.4 copy-start.41
  (21 other events, 36.6 us)
Sparse Core Ops, SparseCore 0:
  81.9 120.9 all-reduce.2
where the time goes:
time: 280 us; the launch traced here: 279 us
  waiting for transfers between devices  132 us (47%)
  other arithmetic  66.1 us (24%)
  local copies, waits for them, and re-layouts  27.4 us (10%)
  matrix products  24 us (9%)
  between operations  16.4 us (6%)
  starting transfers between devices  12.8 us (5%)
    psum x1, waiting for transfers between devices, on_device(): gram_total = lax.psum(gram_local, ('slab', 'grp'))  121 us
    another operation x7, other arithmetic, on_device(): lower_factor = jnp.linalg.cholesky(gram_total)  34.9 us
    another operation x2, other arithmetic, on_device(): lax.linalg.triangular_solve(lower_factor, flat_rows.T, left_side=True, lo...  19.7 us
    dot_general x8, matrix products, on_device(): jnp.einsum('bij,bjr->bir', weights, other_rows, preferred_element_type=jn...  15.4 us
    gather x8, local copies, waits for them, and re-layouts, on_device(): other_rows = jnp.take(row_table, source_ids, axis=0)  12.8 us
    ppermute x4, starting transfers between devices, padded(): after = lax.ppermute(leading, axis, down)  7.73 us
    ppermute x4, waiting for transfers between devices, padded(): before = lax.ppermute(last, axis, up)  7.01 us
  transfers between devices with their start and end apart: 9, of which 5 were waited for; matrix products, arithmetic and copies ran while one was open for 5% of the time, Pallas kernels for 0%

commit v1 on v0

v1 whole, which is shorter than its diff:
```python
import functools
import math

import jax
import jax.numpy as jnp
from jax import lax
from jax.experimental import pallas as pl
from jax.experimental.pallas import tpu as pltpu
from jax.sharding import PartitionSpec as P

MESH = pl.DeviceIdType.MESH
HIGHEST = lax.Precision.HIGHEST
FAR = 100.0
SIDES = [(dz, dy) for dz in (-1, 0, 1) for dy in (-1, 0, 1) if (dz, dy) != (0, 0)]
VMEM = pl.BlockSpec(memory_space=pltpu.VMEM)
SMEM = pl.BlockSpec(memory_space=pltpu.SMEM)


def halo_kernel(slabs, grps, counts, pos, rows, wide_pos, wide_rows, send_p, recv_p, send_r, recv_r, own_sem):
    bz, by, dims, points = pos.shape
    slab, grp = lax.axis_index("slab"), lax.axis_index("grp")
    peers = [
        (lax.rem(slab + dz + slabs, slabs), lax.rem(grp + dy + grps, grps)) for dz, dy in SIDES
    ]
    barrier = pltpu.get_barrier_semaphore()
    for peer in peers:
        pl.semaphore_signal(barrier, inc=1, device_id=peer, device_id_type=MESH)
    own = pltpu.make_async_copy(rows, wide_rows.at[pl.ds(1, bz), pl.ds(1, by)], own_sem)
    own.start()
    ids = lax.broadcasted_iota(jnp.int32, (1, points), 1)
    for a in range(bz):
        for b in range(by):
            here = pos[a, b]
            far = jnp.where(ids < counts[a, b], here[0:1], FAR)
            wide_pos[a + 1, b + 1, 0:1, :] = far
            wide_pos[a + 1, b + 1, 1:3, :] = here[1:3]
            wide_pos[a + 1, b + 1, 3:8, :] = jnp.zeros((5, points), jnp.float32)
    pl.semaphore_wait(barrier, len(SIDES))

    def part(step, length):
        return {-1: (0, 1, length + 1), 0: (0, length, 1), 1: (length - 1, 1, 0)}[step]

    copies = []
    for k, (dz, dy) in enumerate(SIDES):
        z0, zn, zt = part(dz, bz)
        y0, yn, yt = part(dy, by)
        target = (pl.ds(zt, zn), pl.ds(yt, yn))
        copies.append(
            pltpu.make_async_remote_copy(
                src_ref=rows.at[pl.ds(z0, zn), pl.ds(y0, yn)],
                dst_ref=wide_rows.at[target],
                send_sem=send_r.at[k],
                recv_sem=recv_r.at[k],
                device_id=peers[k],
                device_id_type=MESH,
            )
        )
        copies.append(
            pltpu.make_async_remote_copy(
                src_ref=wide_pos.at[pl.ds(z0 + 1, zn), pl.ds(y0 + 1, yn)],
                dst_ref=wide_pos.at[target],
                send_sem=send_p.at[k],
                recv_sem=recv_p.at[k],
                device_id=peers[k],
                device_id_type=MESH,
            )
        )
    for copy in copies:
        copy.start()
    own.wait()
    for copy in copies:
        copy.wait()


def halo(positions, sketch, counts):
    bz, by, _, points = positions.shape
    columns = sketch.shape[3]
    kernel = functools.partial(halo_kernel, lax.axis_size("slab"), lax.axis_size("grp"))
    sides = len(SIDES)
    return pl.pallas_call(
        kernel,
        out_shape=(
            jax.ShapeDtypeStruct((bz + 2, by + 2, 8, points), jnp.float32),
            jax.ShapeDtypeStruct((bz + 2, by + 2, points, columns), sketch.dtype),
        ),
        in_specs=[SMEM, VMEM, VMEM],
        out_specs=(VMEM, VMEM),
        scratch_shapes=[pltpu.SemaphoreType.DMA((sides,))] * 4 + [pltpu.SemaphoreType.DMA],
        compiler_params=pltpu.CompilerParams(
            collective_id=0, has_side_effects=True, vmem_limit_bytes=32 << 20
        ),
        name="halo",
    )(counts, positions, sketch)


def image_kernel(neighbours, wide_pos, wide_rows, image, gram):
    bz, by = wide_pos.shape[0] - 2, wide_pos.shape[1] - 2
    points, columns = wide_rows.shape[2:]
    gram[...] = jnp.zeros_like(gram)

    def block_row(a, carry):
        def block(b, carry):
            own = wide_pos[a + 1, b + 1]
            turned = own.T
            own_z = jnp.where(turned[:, 0:1] > 0.5 * FAR, -FAR, turned[:, 0:1])
            own_y, own_x = turned[:, 1:2], turned[:, 2:3]
            total = jnp.zeros((points, columns), jnp.float32)
            for slot in range(neighbours.shape[2]):
                code = neighbours[a, b, slot]
                step_z = code // 3
                step_y = code - 3 * step_z
                other = wide_pos[a + step_z, b + step_y]
                diff_z = (other[0:1] + (step_z - 1).astype(jnp.float32)) - own_z
                diff_y = (other[1:2] + (step_y - 1).astype(jnp.float32)) - own_y
                diff_x = other[2:3] - own_x
                square = diff_z * diff_z + diff_y * diff_y + diff_x * diff_x
                radius = square * lax.rsqrt(jnp.maximum(square, 1e-30))
                taper = jnp.maximum(1.0 - radius, 0.0)
                taper = taper * taper
                tile = (taper * taper * (4.0 * radius + 1.0)).astype(jnp.bfloat16)
                total = total + jnp.dot(
                    tile, wide_rows[a + step_z, b + step_y], preferred_element_type=jnp.float32
                )
            image[pl.ds((a * by + b) * points, points), :] = total
            return carry

        lax.fori_loop(0, by, block, 0)
        part = image[pl.ds(a * by * points, by * points), :]
        gram[...] += lax.dot_general(
            part, part, (((0,), (0,)), ((), ())), precision=HIGHEST,
            preferred_element_type=jnp.float32,
        )
        return carry

    lax.fori_loop(0, bz, block_row, 0)


def make_image(neighbours, wide_pos, wide_rows):
    bz, by = neighbours.shape[:2]
    points, columns = wide_rows.shape[2:]
    return pl.pallas_call(
        image_kernel,
        out_shape=(
            jax.ShapeDtypeStruct((bz * by * points, columns), jnp.float32),
            jax.ShapeDtypeStruct((columns, columns), jnp.float32),
        ),
        in_specs=[SMEM, VMEM, VMEM],
        out_specs=(VMEM, VMEM),
        compiler_params=pltpu.CompilerParams(vmem_limit_bytes=32 << 20),
        name="image",
    )(neighbours, wide_pos, wide_rows)


def sum_kernel(slabs, grps, gram, out, held_g, part, held_s, *sems):
    n = gram.shape[0]
    wide = n // grps
    owners = min(slabs, wide // 8)
    narrow = wide // owners
    slab, grp = lax.axis_index("slab"), lax.axis_index("grp")
    send_1, recv_1, send_2, recv_2, send_3, recv_3, send_4, recv_4 = sems

    def grp_peer(off):
        return (slab, lax.rem(grp + off, grps))

    def slab_peer(off):
        return (lax.rem(slab + off, slabs), grp)

    barrier = pltpu.get_barrier_semaphore()
    for off in range(1, grps):
        pl.semaphore_signal(barrier, inc=1, device_id=grp_peer(off), device_id_type=MESH)
    for off in range(1, slabs):
        pl.semaphore_signal(barrier, inc=1, device_id=slab_peer(off), device_id_type=MESH)
    pl.semaphore_wait(barrier, grps + slabs - 2)

    def remote(src, dst, send, recv, off, peer):
        return pltpu.make_async_remote_copy(
            src_ref=src, dst_ref=dst, send_sem=send.at[off], recv_sem=recv.at[off],
            device_id=peer, device_id_type=MESH,
        )

    def rows_of(index, size):
        return pl.ds(pl.multiple_of(index * size, size), size)

    first = []
    for off in range(1, grps):
        peer = grp_peer(off)
        first.append(
            remote(gram.at[rows_of(peer[1], wide)], held_g.at[off], send_1, recv_1, off, peer)
        )
    for copy in first:
        copy.start()
    total = gram[rows_of(grp, wide), :]
    for off, copy in enumerate(first, 1):
        copy.wait_recv()
        total = total + held_g[off]
    part[...] = total

    mine = pl.ds(pl.multiple_of(grp * wide, wide), wide)

    def only(condition, body):
        if owners == slabs:
            body()
        else:
            pl.when(condition)(body)

    is_owner = slab < owners
    second = []
    for off in range(1, slabs):
        peer = slab_peer(off)
        place = lax.rem(peer[0], owners)
        second.append(
            remote(part.at[rows_of(place, narrow)], held_s.at[off], send_2, recv_2, off, peer)
        )
        only(peer[0] < owners, second[-1].start)

    place = lax.rem(slab, owners)
    strip = pl.ds(pl.multiple_of(grp * wide + place * narrow, narrow), narrow)
    third = [
        remote(out.at[strip], out.at[strip], send_3, recv_3, off, slab_peer(off))
        for off in range(1, slabs)
    ]

    def add_up():
        total = part[rows_of(place, narrow), :]
        for off, copy in enumerate(second, 1):
            copy.wait_recv()
            total = total + held_s[off]
        out[strip, :] = total
        for copy in third:
            copy.start()

    only(is_owner, add_up)
    for off, copy in enumerate(third, 1):
        only(lax.rem(slab - off + slabs, slabs) < owners, copy.wait_recv)

    fourth = [
        remote(out.at[mine], out.at[mine], send_4, recv_4, off, grp_peer(off))
        for off in range(1, grps)
    ]
    for copy in fourth:
        copy.start()
    for copy in first:
        copy.wait_send()
    for off, copy in enumerate(second, 1):
        only(slab_peer(off)[0] < owners, copy.wait_send)
    for copy in third:
        only(is_owner, copy.wait_send)
    for copy in fourth:
        copy.wait()


def sum_over_devices(gram):
    slabs, grps = lax.axis_size("slab"), lax.axis_size("grp")
    n = gram.shape[0]
    wide = n // grps
    narrow = wide // min(slabs, wide // 8)
    dma = pltpu.SemaphoreType.DMA
    return pl.pallas_call(
        functools.partial(sum_kernel, slabs, grps),
        out_shape=jax.ShapeDtypeStruct((n, n), jnp.float32),
        in_specs=[VMEM],
        out_specs=VMEM,
        scratch_shapes=[
            pltpu.VMEM((grps, wide, n), jnp.float32),
            pltpu.VMEM((wide, n), jnp.float32),
            pltpu.VMEM((slabs, narrow, n), jnp.float32),
        ]
        + [dma((grps,)), dma((grps,))]
        + [dma((slabs,))] * 4
        + [dma((grps,)), dma((grps,))],
        compiler_params=pltpu.CompilerParams(
            collective_id=1, has_side_effects=True, vmem_limit_bytes=32 << 20
        ),
        name="gram_sum",
    )(gram)


HEIGHT = 32
GROUP = 8


def factor_kernel(scale, gram, image, basis, factor, work):
    n = gram.shape[0]
    half = n // 2
    row_ids = lax.broadcasted_iota(jnp.int32, (n, n), 0)
    col_ids = lax.broadcasted_iota(jnp.int32, (n, n), 1)
    work[:, 0:n] = gram[...]
    work[:, n : 2 * n] = jnp.where(row_ids == col_ids, 1.0, 0.0)
    for base in range(0, n, HEIGHT):
        lane0 = 0 if base < half else half
        tiles = [
            work[base : base + HEIGHT, lane0 + half * t : lane0 + half * (t + 1)] for t in range(3)
        ]
        ids = lax.broadcasted_iota(jnp.int32, (HEIGHT, half), 0)
        scales = jnp.zeros((HEIGHT, half), jnp.float32)
        for start in range(0, HEIGHT, GROUP):
            col0 = base - lane0 + start
            spread = [
                jnp.broadcast_to(tiles[0][start:, col0 + j : col0 + j + 1], (HEIGHT - start, half))
                for j in range(GROUP)
            ]
            done = [t[:start] for t in tiles]
            live = [t[start:] for t in tiles]
            live_ids = ids[start:]
            for p in range(GROUP):
                pivot = spread[p][p : p + 1]
                scales = jnp.where(ids == start + p, lax.rsqrt(pivot), scales)
                ratio = jnp.where(live_ids > start + p, spread[p] * (1.0 / pivot), 0.0)
                for j in range(p + 1, GROUP):
                    spread[j] = spread[j] - ratio * spread[j][p : p + 1]
                live = [t - ratio * t[p : p + 1] for t in live]
            tiles = [
                jnp.concatenate([d, t], axis=0) if start else t for d, t in zip(done, live)
            ]
        tiles = [t * scales for t in tiles]
        for t in range(3):
            work[base : base + HEIGHT, lane0 + half * t : lane0 + half * (t + 1)] = tiles[t]
        after = base + HEIGHT
        if after < n:
            right = jnp.concatenate(tiles, axis=1)
            left = jnp.concatenate(tiles[:2], axis=1) if base < half else tiles[0]
            change = lax.dot_general(
                left, right, (((0,), (0,)), ((), ())), precision=HIGHEST,
                preferred_element_type=jnp.float32,
            )
            work[after:n, lane0 : lane0 + 3 * half] -= change[after - lane0 :]
    factor[...] = jnp.where(col_ids >= row_ids, work[:, 0:n], 0.0) * (1.0 / scale)
    inverse = work[:, n : 2 * n] * scale
    rows = image.shape[0]
    chunk = min(rows, 512)

    def solve(i, carry):
        here = pl.ds(pl.multiple_of(i * chunk, chunk), chunk)
        basis[here, :] = lax.dot_general(
            image[here, :], inverse, (((1,), (1,)), ((), ())), precision=HIGHEST,
            preferred_element_type=jnp.float32,
        ).astype(basis.dtype)
        return carry

    lax.fori_loop(0, rows // chunk, solve, 0)


def factor_and_basis(gram, image, scale):
    rows, n = image.shape
    return pl.pallas_call(
        functools.partial(factor_kernel, scale),
        out_shape=(
            jax.ShapeDtypeStruct((rows, n), jnp.bfloat16),
            jax.ShapeDtypeStruct((n, n), jnp.float32),
        ),
        in_specs=[VMEM, VMEM],
        out_specs=(VMEM, VMEM),
        scratch_shapes=[pltpu.VMEM((n, 2 * n), jnp.float32)],
        compiler_params=pltpu.CompilerParams(vmem_limit_bytes=32 << 20),
        name="factor",
    )(gram, image)


def on_device(positions, sketch, counts, neighbours):
    blocks_z, blocks_y, _, points = positions.shape
    columns = sketch.shape[3]
    wide_pos, wide_rows = halo(positions, sketch, counts)
    image, gram = make_image(neighbours, wide_pos, wide_rows)
    gram = sum_over_devices(gram)
    total_rows = lax.axis_size("slab") * blocks_z * lax.axis_size("grp") * blocks_y * points
    basis, factor = factor_and_basis(gram, image, math.sqrt(total_rows))
    return basis.reshape(blocks_z, blocks_y, points, columns), factor


def solution(mesh):
    placed = (
        P("slab", "grp", None, None),
        P("slab", "grp", None, None),
        P("slab", "grp"),
        P("slab", "grp", None),
    )
    return jax.shard_map(
        on_device,
        mesh=mesh,
        in_specs=placed,
        out_specs=(P("slab", "grp", None, None), P()),
        check_vma=False,
    )
```

time: 280 us -> 74.6 us (0.27)
  waiting for transfers between devices: 132 us -> 0 us
  Pallas kernels: 0 us -> 70.3 us
  other arithmetic: 66.1 us -> 0 us
  local copies, waits for them, and re-layouts: 27.4 us -> 3.34 us
  matrix products: 24 us -> 0 us
  between operations: 16.4 us -> 0.67 us
  starting transfers between devices: 12.8 us -> 0 us
    psum x1 -> x0, waiting for transfers between devices: 121 us -> none  [on_device(): gram_total = lax.psum(gram_local, ('slab', 'grp'))]
    pallas_call x0 -> x4, Pallas kernels: none -> 70.3 us  [the longest x1 24.6 us: halo(): pl.pallas_call(kernel, out_shape=(jax.ShapeDtypeStruct((bz + 2, by + 2, 8...]
    another operation x9 -> x0, other arithmetic: 54.5 us -> none  [the longest x7 34.9 us: on_device(): lower_factor = jnp.linalg.cholesky(gram_total)]
    dot_general x9 -> x0, matrix products: 19.5 us -> none  [the longest x8 15.4 us: on_device(): jnp.einsum('bij,bjr->bir', weights, other_rows, preferred_element_type=jn...]
    gather x16 -> x0, local copies, waits for them, and re-layouts: 17.5 us -> none  [the longest x8 12.8 us: on_device(): other_rows = jnp.take(row_table, source_ids, axis=0)]
    ppermute x8 -> x0, starting transfers between devices: 12.8 us -> none  [the longest x4 7.73 us: padded(): after = lax.ppermute(leading, axis, down)]
    ppermute x8 -> x0, waiting for transfers between devices: 10.8 us -> none  [the longest x4 7.01 us: padded(): before = lax.ppermute(last, axis, up)]
    another operation x5 -> x0, matrix products: 4.44 us -> none  [the longest x3 3.97 us: on_device(): lax.linalg.triangular_solve(lower_factor, flat_rows.T, left_side=True, lo...]
  transfers between devices with their start and end apart: 9 -> 0, of which waited for: 5 -> 0; matrix products, arithmetic and copies ran while one was open for 5% -> 0% of each run, Pallas kernels for 0% -> 0%
where the time goes in v1:
time: 74.6 us; the launch traced here: 74.3 us
  Pallas kernels  70.3 us (94%)
  local copies, waits for them, and re-layouts  3.34 us (4%)
    pallas_call x1, Pallas kernels, halo(): pl.pallas_call(kernel, out_shape=(jax.ShapeDtypeStruct((bz + 2, by + 2, 8...  24.6 us
    pallas_call x1, Pallas kernels, sum_over_devices(): pl.pallas_call(functools.partial(sum_kernel, slabs, grps), out_shape=jax....  19.5 us
    pallas_call x1, Pallas kernels, make_image(): pl.pallas_call(image_kernel, out_shape=(jax.ShapeDtypeStruct((bz * by * p...  13.3 us
    pallas_call x1, Pallas kernels, factor_and_basis(): pl.pallas_call(functools.partial(factor_kernel, scale), out_shape=(jax.Sh...  13 us
    unnamed x7, local copies, waits for them, and re-layouts  3.34 us

profile of v1, /device:TPU:1, one launch (start us, length us, event | category | flops | bytes accessed | tf_op | source)
XLA Modules:
  0.0 74.3 jit_solution(10039193709834277780)
XLA Ops:
  0.6 0.8 %copy.6.pos = f32[4,4,3,128]{3,2,1,0:T(4,128)S(1)} copy(f32[4,4,3,128]{3,1,2,0:T(4,128)} %param.4) | data formatting | bytes 49152 | tf_op args[0]
  1.4 0.0 copy-start
  1.4 1.2 %copy-done = bf16[4,4,128,256]{3,2,1,0:T(8,128)(2,1)S(1)} copy-done((bf16[4,4,128,256]{3,2,1,0:T(8,128)(2,1)S(1)}, bf16[4,4,128,256]{3,2,1,0:T(8,128)(2,1)}, u32[]{:S(2)}) %copy-start) | copy-done | bytes 1048600
  2.6 0.0 copy-start.2
  2.6 0.7 copy-done.2
  3.3 24.6 %halo.1 = (f32[6,6,8,128]{3,2,1,0:T(8,128)S(1)}, bf16[6,6,128,256]{3,2,1,0:T(8,128)(2,1)S(1)}) custom-call(s32[4,4]{1,0:T(4,128)S(1)} %copy-done.2, f32[4,4,3,128]{3,2,1,0:T(4,128)S(1)} %copy.6.pos, bf16[4,4,128,256]{3,2,1,0:T(8,128)(2,1)S(1)} %copy-done), custom_call_target="tpu_custom_call" | custom-call | tf_op jit(solution)/shard_map/halo/pallas_call | solution.py:80
  27.9 0.0 copy-start.1
  27.9 0.7 copy-done.1
  28.6 13.3 %image.1 = (f32[2048,256]{1,0:T(8,128)S(1)}, f32[256,256]{1,0:T(8,128)S(1)}) custom-call(s32[4,4,8]{2,1,0:T(4,128)S(1)} %copy-done.1, f32[6,6,8,128]{3,2,1,0:T(8,128)S(1)} %get-tuple-element.8.wide_pos, bf16[6,6,128,256]{3,2,1,0:T(8,128)(2,1)S(1)} %get-tuple-element.9.wide_rows), custom_call_target="tpu_custom_call" | custom-call | tf_op jit(solution)/shard_map/image/pallas_call | solution.py:141
  41.8 19.5 %gram_sum.1.gram = f32[256,256]{1,0:T(8,128)S(1)} custom-call(f32[256,256]{1,0:T(8,128)S(1)} %get-tuple-element.10.gram), custom_call_target="tpu_custom_call" | custom-call | tf_op jit(solution)/shard_map/gram_sum/pallas_call | solution.py:258
  61.3 13.0 %factor.1 = (bf16[2048,256]{1,0:T(8,128)(2,1)}, f32[256,256]{1,0:T(8,128)}) custom-call(f32[256,256]{1,0:T(8,128)S(1)} %gram_sum.1.gram, f32[2048,256]{1,0:T(8,128)S(1)} %get-tuple-element.11.image), custom_call_target="tpu_custom_call" | custom-call | tf_op jit(solution)/shard_map/factor/pallas_call | solution.py:345
Async XLA Ops:
  1.4 1.2 %copy-start = (bf16[4,4,128,256]{3,2,1,0:T(8,128)(2,1)S(1)}, bf16[4,4,128,256]{3,2,1,0:T(8,128)(2,1)}, u32[]{:S(2)}) copy-start(bf16[4,4,128,256]{3,2,1,0:T(8,128)(2,1)} %rows.1) | copy-start | bytes 3145732
  2.6 0.7 copy-start.2
  27.9 0.7 copy-start.1

commit v2 on v1

v2 whole, which is shorter than its diff:
```python
import functools
import math

import jax
import jax.numpy as jnp
from jax import lax
from jax.experimental import pallas as pl
from jax.experimental.pallas import tpu as pltpu
from jax.sharding import PartitionSpec as P

MESH = pl.DeviceIdType.MESH
HIGHEST = lax.Precision.HIGHEST
FAR = 100.0
VMEM = pl.BlockSpec(memory_space=pltpu.VMEM)
SMEM = pl.BlockSpec(memory_space=pltpu.SMEM)


def main_kernel(slabs, grps, counts, neighbours, pos, rows, image, out, wide_pos, wide_rows, cols, gram,
                held_g, part, held_s, own_sem, *sems):
    bz, by, dims, points = pos.shape
    columns = rows.shape[3]
    halo_sems, sems = sems[:8], sems[8:]
    slab, grp = lax.axis_index("slab"), lax.axis_index("grp")

    def grp_peer(off):
        return (slab, lax.rem(grp + off, grps))

    def slab_peer(off):
        return (lax.rem(slab + off, slabs), grp)

    barrier = pltpu.get_barrier_semaphore()
    for off in range(1, grps):
        pl.semaphore_signal(barrier, inc=1, device_id=grp_peer(off), device_id_type=MESH)
    for off in range(1, slabs):
        pl.semaphore_signal(barrier, inc=1, device_id=slab_peer(off), device_id_type=MESH)
    own_rows = pltpu.make_async_copy(rows, wide_rows.at[pl.ds(1, bz), pl.ds(1, by)], own_sem)
    own_rows.start()
    ids = lax.broadcasted_iota(jnp.int32, (1, points), 1)
    for a in range(bz):
        for b in range(by):
            far = jnp.where(ids < counts[a, b], pos[a, b, 0:1], FAR)
            wide_pos[a + 1, b + 1, 0:1, :] = far
            wide_pos[a + 1, b + 1, 1:3, :] = pos[a, b, 1:3]
            wide_pos[a + 1, b + 1, 3:8, :] = jnp.zeros((5, points), jnp.float32)
    own_rows.wait()
    pl.semaphore_wait(barrier, grps + slabs - 2)

    def remote(src, dst, send, recv, peer):
        return pltpu.make_async_remote_copy(
            src_ref=src, dst_ref=dst, send_sem=send, recv_sem=recv,
            device_id=peer, device_id_type=MESH,
        )

    def both(kind, k, src, dst, peer):
        send_r, recv_r, send_p, recv_p = halo_sems[4 * kind : 4 * kind + 4]
        return [
            remote(wide_pos.at[src], wide_pos.at[dst], send_p.at[k], recv_p.at[k], peer),
            remote(wide_rows.at[src], wide_rows.at[dst], send_r.at[k], recv_r.at[k], peer),
        ]

    inner_z, inner_y = pl.ds(1, bz), pl.ds(1, by)
    up, down = slab_peer(1), slab_peer(slabs - 1)
    right, left = grp_peer(1), grp_peer(grps - 1)
    slab_copies = both(0, 0, (pl.ds(bz, 1), inner_y), (pl.ds(0, 1), inner_y), up)
    slab_copies += both(0, 1, (pl.ds(1, 1), inner_y), (pl.ds(bz + 1, 1), inner_y), down)
    grp_copies = both(0, 2, (inner_z, pl.ds(by, 1)), (inner_z, pl.ds(0, 1)), right)
    grp_copies += both(0, 3, (inner_z, pl.ds(1, 1)), (inner_z, pl.ds(by + 1, 1)), left)
    for copy in slab_copies + grp_copies:
        copy.start()

    def turn(i, carry):
        turned = wide_pos[i // by + 1, i % by + 1].T
        own_z = turned[:, 0:1]
        cols[i, 0] = jnp.broadcast_to(jnp.where(own_z > 0.5 * FAR, -FAR, own_z), (points, points))
        cols[i, 1] = jnp.broadcast_to(turned[:, 1:2], (points, points))
        cols[i, 2] = jnp.broadcast_to(turned[:, 2:3], (points, points))
        image[pl.ds(i * points, points), :] = jnp.zeros((points, columns), jnp.float32)
        return carry

    lax.fori_loop(0, bz * by, turn, 0)
    gram[...] = jnp.zeros_like(gram)

    def dropped(a, b):
        total = neighbours[a, b, 0]
        for slot in range(1, neighbours.shape[2]):
            total = total + neighbours[a, b, slot]
        return 36 - total

    def tile(a, b, dz, dy, skip):
        code = 3 * (dz + 1) + dy + 1
        shift_z = jnp.where(skip == code, 10.0 * FAR, jnp.asarray(dz).astype(jnp.float32))
        other = wide_pos[a + dz + 1, b + dy + 1]
        own = a * by + b
        diff_z = (other[0:1] + shift_z) - cols[own, 0]
        diff_y = (other[1:2] + float(dy)) - cols[own, 1]
        diff_x = other[2:3] - cols[own, 2]
        square = diff_z * diff_z + diff_y * diff_y + diff_x * diff_x
        radius = square * lax.rsqrt(jnp.maximum(square, 1e-30))
        taper = jnp.maximum(1.0 - radius, 0.0)
        taper = taper * taper
        return (taper * taper * (4.0 * radius + 1.0)).astype(jnp.bfloat16)

    def add_to(a, b, tiles, sources):
        here = pl.ds((a * by + b) * points, points)
        image[here, :] += jnp.dot(
            jnp.concatenate(tiles, axis=1),
            sources.reshape(len(tiles) * points, columns),
            preferred_element_type=jnp.float32,
        )

    def one_row(t, carry):
        dz, a = t // bz - 1, t % bz
        for b in range(by):
            skip = dropped(a, b)
            steps = [dy for dy in (-1, 0, 1) if 0 <= b + dy < by]
            tiles = [tile(a, b, dz, dy, skip) for dy in steps]
            first = b + steps[0] + 1
            add_to(a, b, tiles, wide_rows[a + dz + 1, first : first + len(steps)])
        return carry

    lax.fori_loop(1, 3 * bz - 1, one_row, 0)

    for copy in slab_copies:
        copy.wait_recv()
    corners = []
    for k, z in enumerate((0, bz + 1)):
        row = pl.ds(z, 1)
        corners += both(1, 2 * k, (row, pl.ds(by, 1)), (row, pl.ds(0, 1)), right)
        corners += both(1, 2 * k + 1, (row, pl.ds(1, 1)), (row, pl.ds(by + 1, 1)), left)
    for copy in corners:
        copy.start()

    lax.fori_loop(0, 2, lambda i, carry: one_row(i * (3 * bz - 1), carry), 0)

    for copy in grp_copies + corners:
        copy.wait_recv()

    def outer(a, carry):
        for b, dy in ((0, -1), (by - 1, 1)):
            skip = dropped(a, b)
            tiles = [tile(a, b, dz, dy, skip) for dz in (-1, 0, 1)]
            add_to(a, b, tiles, wide_rows[pl.ds(a, 3), b + dy + 1])
        band = image[pl.ds(a * by * points, by * points), :]
        gram[...] += lax.dot_general(
            band, band, (((0,), (0,)), ((), ())), precision=HIGHEST,
            preferred_element_type=jnp.float32,
        )
        return carry

    lax.fori_loop(0, bz, outer, 0)
    sum_gram(slabs, grps, slab, grp, grp_peer, slab_peer, gram, out, held_g, part, held_s, sems)
    for copy in slab_copies + grp_copies + corners:
        copy.wait_send()


def sum_gram(slabs, grps, slab, grp, grp_peer, slab_peer, gram, out, held_g, part, held_s, sems):
    n = gram.shape[0]
    wide = n // grps
    owners = min(slabs, wide // 8)
    narrow = wide // owners
    send_1, recv_1, send_2, recv_2, send_3, recv_3, send_4, recv_4 = sems

    def remote(src, dst, send, recv, off, peer):
        return pltpu.make_async_remote_copy(
            src_ref=src, dst_ref=dst, send_sem=send.at[off], recv_sem=recv.at[off],
            device_id=peer, device_id_type=MESH,
        )

    def rows_of(index, size):
        return pl.ds(pl.multiple_of(index * size, size), size)

    first = []
    for off in range(1, grps):
        peer = grp_peer(off)
        first.append(
            remote(gram.at[rows_of(peer[1], wide)], held_g.at[off], send_1, recv_1, off, peer)
        )
    for copy in first:
        copy.start()
    total = gram[rows_of(grp, wide), :]
    for off, copy in enumerate(first, 1):
        copy.wait_recv()
        total = total + held_g[off]
    part[...] = total

    mine = pl.ds(pl.multiple_of(grp * wide, wide), wide)

    def only(condition, body):
        if owners == slabs:
            body()
        else:
            pl.when(condition)(body)

    is_owner = slab < owners
    second = []
    for off in range(1, slabs):
        peer = slab_peer(off)
        place = lax.rem(peer[0], owners)
        second.append(
            remote(part.at[rows_of(place, narrow)], held_s.at[off], send_2, recv_2, off, peer)
        )
        only(peer[0] < owners, second[-1].start)

    place = lax.rem(slab, owners)
    strip = pl.ds(pl.multiple_of(grp * wide + place * narrow, narrow), narrow)
    third = [
        remote(out.at[strip], out.at[strip], send_3, recv_3, off, slab_peer(off))
        for off in range(1, slabs)
    ]

    def add_up():
        total = part[rows_of(place, narrow), :]
        for off, copy in enumerate(second, 1):
            copy.wait_recv()
            total = total + held_s[off]
        out[strip, :] = total
        for copy in third:
            copy.start()

    only(is_owner, add_up)
    for off, copy in enumerate(third, 1):
        only(lax.rem(slab - off + slabs, slabs) < owners, copy.wait_recv)

    fourth = [
        remote(out.at[mine], out.at[mine], send_4, recv_4, off, grp_peer(off))
        for off in range(1, grps)
    ]
    for copy in fourth:
        copy.start()
    for copy in first:
        copy.wait_send()
    for off, copy in enumerate(second, 1):
        only(slab_peer(off)[0] < owners, copy.wait_send)
    for copy in third:
        only(is_owner, copy.wait_send)
    for copy in fourth:
        copy.wait()


def image_and_gram(positions, sketch, counts, neighbours):
    slabs, grps = lax.axis_size("slab"), lax.axis_size("grp")
    bz, by, _, points = positions.shape
    n = sketch.shape[3]
    wide = n // grps
    narrow = wide // min(slabs, wide // 8)
    dma = pltpu.SemaphoreType.DMA
    vmem = pltpu.VMEM
    return pl.pallas_call(
        functools.partial(main_kernel, slabs, grps),
        out_shape=(
            jax.ShapeDtypeStruct((bz * by * points, n), jnp.float32),
            jax.ShapeDtypeStruct((n, n), jnp.float32),
        ),
        in_specs=[SMEM, SMEM, VMEM, pl.BlockSpec(memory_space=pl.ANY)],
        out_specs=(VMEM, VMEM),
        scratch_shapes=[
            vmem((bz + 2, by + 2, 8, points), jnp.float32),
            vmem((bz + 2, by + 2, points, n), sketch.dtype),
            vmem((bz * by, 3, points, points), jnp.float32),
            vmem((n, n), jnp.float32),
            vmem((grps, wide, n), jnp.float32),
            vmem((wide, n), jnp.float32),
            vmem((slabs, narrow, n), jnp.float32),
            dma,
        ]
        + [dma((4,))] * 8
        + [dma((grps,)), dma((grps,))]
        + [dma((slabs,))] * 4
        + [dma((grps,)), dma((grps,))],
        compiler_params=pltpu.CompilerParams(
            collective_id=0, has_side_effects=True, vmem_limit_bytes=40 << 20
        ),
        name="image_gram",
    )(counts, neighbours, positions, sketch)


HEIGHT = 32
GROUP = 8


def factor_kernel(scale, gram, image, basis, factor, work):
    n = gram.shape[0]
    half = n // 2
    row_ids = lax.broadcasted_iota(jnp.int32, (n, n), 0)
    col_ids = lax.broadcasted_iota(jnp.int32, (n, n), 1)
    work[:, 0:n] = gram[...]
    work[:, n : 2 * n] = jnp.where(row_ids == col_ids, 1.0, 0.0)
    for base in range(0, n, HEIGHT):
        lane0 = 0 if base < half else half
        tiles = [
            work[base : base + HEIGHT, lane0 + half * t : lane0 + half * (t + 1)] for t in range(3)
        ]
        ids = lax.broadcasted_iota(jnp.int32, (HEIGHT, half), 0)
        scales = jnp.zeros((HEIGHT, half), jnp.float32)
        for start in range(0, HEIGHT, GROUP):
            col0 = base - lane0 + start
            spread = [
                jnp.broadcast_to(tiles[0][start:, col0 + j : col0 + j + 1], (HEIGHT - start, half))
                for j in range(GROUP)
            ]
            done = [t[:start] for t in tiles]
            live = [t[start:] for t in tiles]
            live_ids = ids[start:]
            for p in range(GROUP):
                pivot = spread[p][p : p + 1]
                scales = jnp.where(ids == start + p, lax.rsqrt(pivot), scales)
                ratio = jnp.where(live_ids > start + p, spread[p] * (1.0 / pivot), 0.0)
                for j in range(p + 1, GROUP):
                    spread[j] = spread[j] - ratio * spread[j][p : p + 1]
                live = [t - ratio * t[p : p + 1] for t in live]
            tiles = [
                jnp.concatenate([d, t], axis=0) if start else t for d, t in zip(done, live)
            ]
        tiles = [t * scales for t in tiles]
        for t in range(3):
            work[base : base + HEIGHT, lane0 + half * t : lane0 + half * (t + 1)] = tiles[t]
        after = base + HEIGHT
        if after < n:
            right = jnp.concatenate(tiles, axis=1)
            left = jnp.concatenate(tiles[:2], axis=1) if base < half else tiles[0]
            change = lax.dot_general(
                left, right, (((0,), (0,)), ((), ())), precision=HIGHEST,
                preferred_element_type=jnp.float32,
            )
            work[after:n, lane0 : lane0 + 3 * half] -= change[after - lane0 :]
    factor[...] = jnp.where(col_ids >= row_ids, work[:, 0:n], 0.0) * (1.0 / scale)
    inverse = work[:, n : 2 * n] * scale
    rows = image.shape[0]
    chunk = min(rows, 512)

    def solve(i, carry):
        here = pl.ds(pl.multiple_of(i * chunk, chunk), chunk)
        basis[here, :] = lax.dot_general(
            image[here, :], inverse, (((1,), (1,)), ((), ())), precision=HIGHEST,
            preferred_element_type=jnp.float32,
        ).astype(basis.dtype)
        return carry

    lax.fori_loop(0, rows // chunk, solve, 0)


def factor_and_basis(gram, image, scale):
    rows, n = image.shape
    return pl.pallas_call(
        functools.partial(factor_kernel, scale),
        out_shape=(
            jax.ShapeDtypeStruct((rows, n), jnp.bfloat16),
            jax.ShapeDtypeStruct((n, n), jnp.float32),
        ),
        in_specs=[VMEM, VMEM],
        out_specs=(VMEM, VMEM),
        scratch_shapes=[pltpu.VMEM((n, 2 * n), jnp.float32)],
        compiler_params=pltpu.CompilerParams(vmem_limit_bytes=32 << 20),
        name="factor",
    )(gram, image)


def on_device(positions, sketch, counts, neighbours):
    blocks_z, blocks_y, _, points = positions.shape
    columns = sketch.shape[3]
    image, gram = image_and_gram(positions, sketch, counts, neighbours)
    total_rows = lax.axis_size("slab") * blocks_z * lax.axis_size("grp") * blocks_y * points
    basis, factor = factor_and_basis(gram, image, math.sqrt(total_rows))
    return basis.reshape(blocks_z, blocks_y, points, columns), factor


def solution(mesh):
    placed = (
        P("slab", "grp", None, None),
        P("slab", "grp", None, None),
        P("slab", "grp"),
        P("slab", "grp", None),
    )
    return jax.shard_map(
        on_device,
        mesh=mesh,
        in_specs=placed,
        out_specs=(P("slab", "grp", None, None), P()),
        check_vma=False,
    )
```

time: 74.6 us -> 63 us (0.84)
  Pallas kernels: 70.3 us -> 58.7 us
    pallas_call x3 -> x1, Pallas kernels: 57.3 us -> 45.7 us  [image_and_gram(): pl.pallas_call(functools.partial(main_kernel, slabs, grps), out_shape=(ja...]
where the time goes in v2:
time: 63 us; the launch traced here: 62.7 us
  Pallas kernels  58.7 us (93%)
  local copies, waits for them, and re-layouts  3.35 us (5%)
  between operations  0.65 us (1%)
    pallas_call x1, Pallas kernels, image_and_gram(): pl.pallas_call(functools.partial(main_kernel, slabs, grps), out_shape=(ja...  45.7 us
    pallas_call x1, Pallas kernels, factor_and_basis(): pl.pallas_call(functools.partial(factor_kernel, scale), out_shape=(jax.Sh...  13 us
    unnamed x7, local copies, waits for them, and re-layouts  3.35 us

profile of v2, /device:TPU:1, one launch (start us, length us, event | category | flops | bytes accessed | tf_op | source)
XLA Modules:
  0.0 62.7 jit_solution(12226205896496906018)
XLA Ops:
  0.6 0.8 %copy.6.pos = f32[4,4,3,128]{3,2,1,0:T(4,128)S(1)} copy(f32[4,4,3,128]{3,1,2,0:T(4,128)} %param.4) | data formatting | bytes 49152 | tf_op args[0]
  1.4 0.0 copy-start
  1.4 1.2 %copy-done = bf16[4,4,128,256]{3,2,1,0:T(8,128)(2,1)S(1)} copy-done((bf16[4,4,128,256]{3,2,1,0:T(8,128)(2,1)S(1)}, bf16[4,4,128,256]{3,2,1,0:T(8,128)(2,1)}, u32[]{:S(2)}) %copy-start) | copy-done | bytes 1048600
  2.6 0.0 copy-start.1
  2.6 0.7 %copy-done.1 = s32[4,4,8]{2,1,0:T(4,128)S(1)} copy-done((s32[4,4,8]{2,1,0:T(4,128)S(1)}, s32[4,4,8]{2,1,0:T(4,128)}, u32[]{:S(2)}) %copy-start.1) | copy-done | bytes 536
  3.3 0.0 copy-start.2
  3.3 0.7 %copy-done.2 = s32[4,4]{1,0:T(4,128)S(1)} copy-done((s32[4,4]{1,0:T(4,128)S(1)}, s32[4,4]{1,0:T(4,128)}, u32[]{:S(2)}) %copy-start.2) | copy-done | bytes 88
  4.0 45.7 %image_gram.1 = (f32[2048,256]{1,0:T(8,128)S(1)}, f32[256,256]{1,0:T(8,128)S(1)}) custom-call(s32[4,4]{1,0:T(4,128)S(1)} %copy-done.2, s32[4,4,8]{2,1,0:T(4,128)S(1)} %copy-done.1, f32[4,4,3,128]{3,2,1,0:T(4,128)S(1)} %copy.6.pos, bf16[4,4,128,256]{3,2,1,0:T(8,128)(2,1)S(1)} %copy-done), custom_call_target="tpu_custom_call" | custom-call | tf_op jit(solution)/shard_map/image_gram/pallas_call | solution.py:248
  49.7 13.0 %factor.1 = (bf16[2048,256]{1,0:T(8,128)(2,1)}, f32[256,256]{1,0:T(8,128)}) custom-call(f32[256,256]{1,0:T(8,128)S(1)} %get-tuple-element.6.gram, f32[2048,256]{1,0:T(8,128)S(1)} %get-tuple-element.7.image), custom_call_target="tpu_custom_call" | custom-call | tf_op jit(solution)/shard_map/factor/pallas_call | solution.py:344
Async XLA Ops:
  1.4 1.2 %copy-start = (bf16[4,4,128,256]{3,2,1,0:T(8,128)(2,1)S(1)}, bf16[4,4,128,256]{3,2,1,0:T(8,128)(2,1)}, u32[]{:S(2)}) copy-start(bf16[4,4,128,256]{3,2,1,0:T(8,128)(2,1)} %rows.1) | copy-start | bytes 3145732
  2.6 0.7 %copy-start.1 = (s32[4,4,8]{2,1,0:T(4,128)S(1)}, s32[4,4,8]{2,1,0:T(4,128)}, u32[]{:S(2)}) copy-start(s32[4,4,8]{2,1,0:T(4,128)} %neighbours.1) | copy-start | bytes 1540
  3.3 0.7 %copy-start.2 = (s32[4,4]{1,0:T(4,128)S(1)}, s32[4,4]{1,0:T(4,128)}, u32[]{:S(2)}) copy-start(s32[4,4]{1,0:T(4,128)} %counts.1) | copy-start | bytes 196

commit v3 on v2

--- a/solution.py
+++ b/solution.py
@@ -15,7 +15,20 @@
 SMEM = pl.BlockSpec(memory_space=pltpu.SMEM)
 
 
-def main_kernel(slabs, grps, counts, neighbours, pos, rows, image, out, wide_pos, wide_rows, cols, gram,
+def two_parts(x):
+    high = x.astype(jnp.bfloat16)
+    return high, (x - high.astype(jnp.float32)).astype(jnp.bfloat16)
+
+
+def turned_dot(x, y):
+    return lax.dot_general(x, y, (((0,), (0,)), ((), ())), preferred_element_type=jnp.float32)
+
+
+def dot_turned(x, y):
+    return lax.dot_general(x, y, (((1,), (1,)), ((), ())), preferred_element_type=jnp.float32)
+
+
+def main_kernel(slabs, grps, counts, neighbours, pos, rows, image, out, wide_pos, wide_rows, own_parts, other_parts, gram, cross,
                 held_g, part, held_s, own_sem, *sems):
     bz, by, dims, points = pos.shape
     columns = rows.shape[3]
@@ -61,24 +74,55 @@
     inner_z, inner_y = pl.ds(1, bz), pl.ds(1, by)
     up, down = slab_peer(1), slab_peer(slabs - 1)
     right, left = grp_peer(1), grp_peer(grps - 1)
-    slab_copies = both(0, 0, (pl.ds(bz, 1), inner_y), (pl.ds(0, 1), inner_y), up)
-    slab_copies += both(0, 1, (pl.ds(1, 1), inner_y), (pl.ds(bz + 1, 1), inner_y), down)
-    grp_copies = both(0, 2, (inner_z, pl.ds(by, 1)), (inner_z, pl.ds(0, 1)), right)
-    grp_copies += both(0, 3, (inner_z, pl.ds(1, 1)), (inner_z, pl.ds(by + 1, 1)), left)
-    for copy in slab_copies + grp_copies:
+    ends, middles = [], []
+    for k, source, target, peer in ((0, bz, 0, up), (3, 1, bz + 1, down)):
+        for at, copies, y in (
+            (0, ends, pl.ds(1, 1)), (1, ends, pl.ds(by, 1)), (2, middles, pl.ds(2, by - 2))
+        ):
+            copies += both(0, k + at, (pl.ds(source, 1), y), (pl.ds(target, 1), y), peer)
+    grp_copies = both(0, 6, (inner_z, pl.ds(by, 1)), (inner_z, pl.ds(0, 1)), right)
+    grp_copies += both(0, 7, (inner_z, pl.ds(1, 1)), (inner_z, pl.ds(by + 1, 1)), left)
+    for copy in ends + middles + grp_copies:
         copy.start()
 
-    def turn(i, carry):
-        turned = wide_pos[i // by + 1, i % by + 1].T
-        own_z = turned[:, 0:1]
-        cols[i, 0] = jnp.broadcast_to(jnp.where(own_z > 0.5 * FAR, -FAR, own_z), (points, points))
-        cols[i, 1] = jnp.broadcast_to(turned[:, 1:2], (points, points))
-        cols[i, 2] = jnp.broadcast_to(turned[:, 2:3], (points, points))
-        image[pl.ds(i * points, points), :] = jnp.zeros((points, columns), jnp.float32)
+    part_rows = lax.broadcasted_iota(jnp.int32, (8, points), 0)
+
+    def split(z, y):
+        here = wide_pos[z, y]
+        mid_z = (jnp.asarray(z) - 1 - bz // 2).astype(jnp.float32)
+        mid_y = (jnp.asarray(y) - 1 - by // 2).astype(jnp.float32)
+        moved = here + jnp.where(part_rows == 0, mid_z, jnp.where(part_rows == 1, mid_y, -0.5))
+        empty = here[0:1] > 0.5 * FAR
+        moved = jnp.where((part_rows < 3) & jnp.logical_not(empty), moved, 0.0)
+        norm = jnp.where(empty, 1000.0, jnp.sum(moved * moved, axis=0, keepdims=True))
+        whole = jnp.where(part_rows == 3, norm, moved)
+        high = whole.astype(jnp.bfloat16).astype(jnp.float32)
+        rest = whole - high
+        middle = rest.astype(jnp.bfloat16).astype(jnp.float32)
+        return high, middle, rest - middle
+
+    def stack(parts, norms):
+        merged = [jnp.where(part_rows == 3, n, p) for p, n in zip(parts, norms)]
+        return jnp.concatenate(merged, axis=0)
+
+    def put_other(z, y):
+        h, m, low = split(z, y)
+        parts = [-2.0 * p for p in (h, m, h, m, low, h)]
+        other_parts[z, y] = stack(parts, (1.0, 1.0, 1.0, h, m, low)).astype(jnp.bfloat16)
+        return h, m, low
+
+    def turn(a, carry):
+        for b in range(by):
+            h, m, low = put_other(a + 1, b + 1)
+            mine = stack((h, h, m, m, h, low), (h, m, low, 1.0, 1.0, 1.0))
+            own_parts[a * by + b] = mine.T.astype(jnp.bfloat16)
+        band = pl.ds(a * by * points, by * points)
+        image[band, :] = jnp.zeros((by * points, columns), jnp.float32)
         return carry
 
-    lax.fori_loop(0, bz * by, turn, 0)
+    lax.fori_loop(0, bz, turn, 0)
     gram[...] = jnp.zeros_like(gram)
+    cross[...] = jnp.zeros_like(cross)
 
     def dropped(a, b):
         total = neighbours[a, b, 0]
@@ -88,14 +132,13 @@
 
     def tile(a, b, dz, dy, skip):
         code = 3 * (dz + 1) + dy + 1
-        shift_z = jnp.where(skip == code, 10.0 * FAR, jnp.asarray(dz).astype(jnp.float32))
-        other = wide_pos[a + dz + 1, b + dy + 1]
-        own = a * by + b
-        diff_z = (other[0:1] + shift_z) - cols[own, 0]
-        diff_y = (other[1:2] + float(dy)) - cols[own, 1]
-        diff_x = other[2:3] - cols[own, 2]
-        square = diff_z * diff_z + diff_y * diff_y + diff_x * diff_x
-        radius = square * lax.rsqrt(jnp.maximum(square, 1e-30))
+        least = jnp.where(skip == code, 4.0, 1e-30)
+        square = jnp.dot(
+            own_parts[a * by + b], other_parts[a + dz + 1, b + dy + 1],
+            preferred_element_type=jnp.float32,
+        )
+        square = jnp.maximum(square, least)
+        radius = square * lax.rsqrt(square)
         taper = jnp.maximum(1.0 - radius, 0.0)
         taper = taper * taper
         return (taper * taper * (4.0 * radius + 1.0)).astype(jnp.bfloat16)
@@ -118,9 +161,9 @@
             add_to(a, b, tiles, wide_rows[a + dz + 1, first : first + len(steps)])
         return carry
 
-    lax.fori_loop(1, 3 * bz - 1, one_row, 0)
-
-    for copy in slab_copies:
+    lax.fori_loop(1, bz + 1, one_row, 0)
+
+    for copy in ends:
         copy.wait_recv()
     corners = []
     for k, z in enumerate((0, bz + 1)):
@@ -129,11 +172,21 @@
         corners += both(1, 2 * k + 1, (row, pl.ds(1, 1)), (row, pl.ds(by + 1, 1)), left)
     for copy in corners:
         copy.start()
+    lax.fori_loop(bz + 1, 3 * bz - 1, one_row, 0)
+
+    for copy in middles:
+        copy.wait_recv()
+    for y in range(1, by + 1):
+        put_other(0, y)
+        put_other(bz + 1, y)
 
     lax.fori_loop(0, 2, lambda i, carry: one_row(i * (3 * bz - 1), carry), 0)
 
     for copy in grp_copies + corners:
         copy.wait_recv()
+    for z in range(bz + 2):
+        put_other(z, 0)
+        put_other(z, by + 1)
 
     def outer(a, carry):
         for b, dy in ((0, -1), (by - 1, 1)):
@@ -141,15 +194,15 @@
             tiles = [tile(a, b, dz, dy, skip) for dz in (-1, 0, 1)]
             add_to(a, b, tiles, wide_rows[pl.ds(a, 3), b + dy + 1])
         band = image[pl.ds(a * by * points, by * points), :]
-        gram[...] += lax.dot_general(
-            band, band, (((0,), (0,)), ((), ())), precision=HIGHEST,
-            preferred_element_type=jnp.float32,
-        )
+        high, low = two_parts(band)
+        gram[...] += turned_dot(high, high) + turned_dot(low, low)
+        cross[...] += turned_dot(high, low)
         return carry
 
     lax.fori_loop(0, bz, outer, 0)
+    gram[...] += cross[...] + cross[...].T
     sum_gram(slabs, grps, slab, grp, grp_peer, slab_peer, gram, out, held_g, part, held_s, sems)
-    for copy in slab_copies + grp_copies + corners:
+    for copy in ends + middles + grp_copies + corners:
         copy.wait_send()
 
 
@@ -256,14 +309,16 @@
         scratch_shapes=[
             vmem((bz + 2, by + 2, 8, points), jnp.float32),
             vmem((bz + 2, by + 2, points, n), sketch.dtype),
-            vmem((bz * by, 3, points, points), jnp.float32),
+            vmem((bz * by, points, 48), jnp.bfloat16),
+            vmem((bz + 2, by + 2, 48, points), jnp.bfloat16),
+            vmem((n, n), jnp.float32),
             vmem((n, n), jnp.float32),
             vmem((grps, wide, n), jnp.float32),
             vmem((wide, n), jnp.float32),
             vmem((slabs, narrow, n), jnp.float32),
             dma,
         ]
-        + [dma((4,))] * 8
+        + [dma((8,))] * 8
         + [dma((grps,)), dma((grps,))]
         + [dma((slabs,))] * 4
         + [dma((grps,)), dma((grps,))],
@@ -274,7 +329,7 @@
     )(counts, neighbours, positions, sketch)
 
 
-HEIGHT = 32
+HEIGHT = 64
 GROUP = 8
 
 
@@ -324,16 +379,15 @@
             )
             work[after:n, lane0 : lane0 + 3 * half] -= change[after - lane0 :]
     factor[...] = jnp.where(col_ids >= row_ids, work[:, 0:n], 0.0) * (1.0 / scale)
-    inverse = work[:, n : 2 * n] * scale
+    inverse_high, inverse_low = two_parts(work[:, n : 2 * n] * scale)
     rows = image.shape[0]
     chunk = min(rows, 512)
 
     def solve(i, carry):
         here = pl.ds(pl.multiple_of(i * chunk, chunk), chunk)
-        basis[here, :] = lax.dot_general(
-            image[here, :], inverse, (((1,), (1,)), ((), ())), precision=HIGHEST,
-            preferred_element_type=jnp.float32,
-        ).astype(basis.dtype)
+        high, low = two_parts(image[here, :])
+        solved = dot_turned(high, inverse_high) + dot_turned(high, inverse_low)
+        basis[here, :] = (solved + dot_turned(low, inverse_high)).astype(basis.dtype)
         return carry
 
     lax.fori_loop(0, rows // chunk, solve, 0)

time: 63 us -> 58.1 us (0.922)
  Pallas kernels: 58.7 us -> 53.9 us
    pallas_call x1, Pallas kernels: 45.7 us -> 43 us  [image_and_gram(): pl.pallas_call(functools.partial(main_kernel, slabs, grps), out_shape=(ja...]
    pallas_call x1, Pallas kernels: 13 us -> 10.8 us  [factor_and_basis(): pl.pallas_call(functools.partial(factor_kernel, scale), out_shape=(jax.Sh...]
where the time goes in v3:
time: 58.1 us; the launch traced here: 57.9 us
  Pallas kernels  53.9 us (93%)
  local copies, waits for them, and re-layouts  3.35 us (6%)
  between operations  0.65 us (1%)
    pallas_call x1, Pallas kernels, image_and_gram(): pl.pallas_call(functools.partial(main_kernel, slabs, grps), out_shape=(ja...  43 us
    pallas_call x1, Pallas kernels, factor_and_basis(): pl.pallas_call(functools.partial(factor_kernel, scale), out_shape=(jax.Sh...  10.8 us
    unnamed x7, local copies, waits for them, and re-layouts  3.35 us

profile of v3, /device:TPU:1, one launch (start us, length us, event | category | flops | bytes accessed | tf_op | source)
XLA Modules:
  0.0 57.9 jit_solution(16089715969310490186)
XLA Ops:
  0.6 0.8 %copy.6.pos = f32[4,4,3,128]{3,2,1,0:T(4,128)S(1)} copy(f32[4,4,3,128]{3,1,2,0:T(4,128)} %param.4) | data formatting | bytes 49152 | tf_op args[0]
  1.4 0.0 copy-start
  1.4 1.2 %copy-done = bf16[4,4,128,256]{3,2,1,0:T(8,128)(2,1)S(1)} copy-done((bf16[4,4,128,256]{3,2,1,0:T(8,128)(2,1)S(1)}, bf16[4,4,128,256]{3,2,1,0:T(8,128)(2,1)}, u32[]{:S(2)}) %copy-start) | copy-done | bytes 1048600
  2.6 0.0 copy-start.1
  2.6 0.7 %copy-done.1 = s32[4,4,8]{2,1,0:T(4,128)S(1)} copy-done((s32[4,4,8]{2,1,0:T(4,128)S(1)}, s32[4,4,8]{2,1,0:T(4,128)}, u32[]{:S(2)}) %copy-start.1) | copy-done | bytes 536
  3.3 0.0 copy-start.2
  3.3 0.7 %copy-done.2 = s32[4,4]{1,0:T(4,128)S(1)} copy-done((s32[4,4]{1,0:T(4,128)S(1)}, s32[4,4]{1,0:T(4,128)}, u32[]{:S(2)}) %copy-start.2) | copy-done | bytes 88
  4.0 43.0 %image_gram.1 = (f32[2048,256]{1,0:T(8,128)S(1)}, f32[256,256]{1,0:T(8,128)S(1)}) custom-call(s32[4,4]{1,0:T(4,128)S(1)} %copy-done.2, s32[4,4,8]{2,1,0:T(4,128)S(1)} %copy-done.1, f32[4,4,3,128]{3,2,1,0:T(4,128)S(1)} %copy.6.pos, bf16[4,4,128,256]{3,2,1,0:T(8,128)(2,1)S(1)} %copy-done), custom_call_target="tpu_custom_call" | custom-call | tf_op jit(solution)/shard_map/image_gram/pallas_call | solution.py:301
  47.0 10.8 %factor.1 = (bf16[2048,256]{1,0:T(8,128)(2,1)}, f32[256,256]{1,0:T(8,128)}) custom-call(f32[256,256]{1,0:T(8,128)S(1)} %get-tuple-element.6.gram, f32[2048,256]{1,0:T(8,128)S(1)} %get-tuple-element.7.image), custom_call_target="tpu_custom_call" | custom-call | tf_op jit(solution)/shard_map/factor/pallas_call | solution.py:398
Async XLA Ops:
  1.4 1.2 %copy-start = (bf16[4,4,128,256]{3,2,1,0:T(8,128)(2,1)S(1)}, bf16[4,4,128,256]{3,2,1,0:T(8,128)(2,1)}, u32[]{:S(2)}) copy-start(bf16[4,4,128,256]{3,2,1,0:T(8,128)(2,1)} %rows.1) | copy-start | bytes 3145732
  2.6 0.7 %copy-start.1 = (s32[4,4,8]{2,1,0:T(4,128)S(1)}, s32[4,4,8]{2,1,0:T(4,128)}, u32[]{:S(2)}) copy-start(s32[4,4,8]{2,1,0:T(4,128)} %neighbours.1) | copy-start | bytes 1540
  3.3 0.7 %copy-start.2 = (s32[4,4]{1,0:T(4,128)S(1)}, s32[4,4]{1,0:T(4,128)}, u32[]{:S(2)}) copy-start(s32[4,4]{1,0:T(4,128)} %counts.1) | copy-start | bytes 196
